TPU v7x, 32 devices: a whole 2x2x4 slice. The times are simulated.
32 devices in a mesh: row: 4 (over y, core), col: 4 (over z), feat: 2 (over x).
Axes of the slice: x: 2, y: 2, z: 4, core: 2. Of those that a mesh axis runs over, the one named last changes fastest.
Arguments:
- panel_student: bfloat16 [2048, 4096], P('row', 'feat'), may hold values from -0.01171875 to 0.01171875
- panel_teacher: bfloat16 [2048, 4096], P('row', 'feat'), may hold values from -0.01171875 to 0.01171875
- tokens_student: bfloat16 [3072, 4096], P('col', 'feat'), may hold values from -0.01171875 to 0.01171875
- tokens_teacher: bfloat16 [3072, 4096], P('col', 'feat'), may hold values from -0.01171875 to 0.01171875
Outputs:
- row_loss: float32 [2048], P(('row', 'col'))
- grad_panel: bfloat16 [2048, 4096], P(('row', 'col'), 'feat')
- grad_tokens: bfloat16 [3072, 4096], P('col', 'feat')
All inputs are finite; a program needn't handle non-finite values.
Results may differ from a plain program's by a relative error of at most 0.0058.
Values may be sent and summed in bfloat16 or wider, within the bound.
A program may use at most 128 MiB of HBM per device.

v0:
```python
import jax
import jax.numpy as jnp
from jax import lax
from jax.sharding import PartitionSpec as P

epsilon = 1e-06


def squares(features):
    values = features.astype(jnp.float32)
    return jnp.sum(values * values, axis=1)


def inner(left, right):
    return jnp.einsum("rd,cd->rc", left, right, preferred_element_type=jnp.float32)


def inverse(total):
    return 1.0 / jnp.sqrt(total + epsilon)


def local(panel_student, panel_teacher, tokens_student, tokens_teacher):
    student_dots, teacher_dots, sq_ps, sq_pt, sq_ts, sq_tt = lax.psum(
        (
            inner(panel_student, tokens_student),
            inner(panel_teacher, tokens_teacher),
            squares(panel_student),
            squares(panel_teacher),
            squares(tokens_student),
            squares(tokens_teacher),
        ),
        "feat",
    )
    inv_ps = inverse(sq_ps)
    inv_pt = inverse(sq_pt)
    inv_ts = inverse(sq_ts)
    inv_tt = inverse(sq_tt)
    student_gram = student_dots * inv_ps[:, None] * inv_ts[None, :]
    teacher_gram = teacher_dots * inv_pt[:, None] * inv_tt[None, :]
    mismatch = student_gram - teacher_gram
    loss_part = jnp.sum(mismatch * mismatch, axis=1)
    doubled = (2.0 * mismatch).astype(jnp.bfloat16)
    panel_unit = panel_student.astype(jnp.float32) * inv_ps[:, None]
    token_unit = tokens_student.astype(jnp.float32) * inv_ts[:, None]
    panel_half = panel_unit.astype(jnp.bfloat16)
    token_half = token_unit.astype(jnp.bfloat16)
    panel_part = jnp.dot(doubled, token_half, preferred_element_type=jnp.float32)
    panel_term, row_loss = (
        lax.psum_scatter(panel_part, "col", scatter_dimension=0, tiled=True),
        lax.psum_scatter(loss_part, "col", scatter_dimension=0, tiled=True),
    )
    token_part = jnp.einsum("rc,rd->cd", doubled, panel_half, preferred_element_type=jnp.float32)
    token_term = lax.psum_scatter(token_part, "row", scatter_dimension=0, tiled=True)
    col_share = tokens_student.shape[0] // lax.axis_size("row")
    col_offset = lax.axis_index("row") * col_share
    unit_cols = lax.dynamic_slice_in_dim(token_unit, col_offset, col_share, 0)
    inv_cols = lax.dynamic_slice_in_dim(inv_ts, col_offset, col_share, 0)
    share = panel_student.shape[0] // lax.axis_size("col")
    offset = lax.axis_index("col") * share
    unit_rows = lax.dynamic_slice_in_dim(panel_unit, offset, share, 0)
    inv_rows = lax.dynamic_slice_in_dim(inv_ps, offset, share, 0)
    along_panel, along_tokens = lax.psum(
        (jnp.sum(unit_rows * panel_term, axis=1), jnp.sum(unit_cols * token_term, axis=1)), "feat"
    )
    grad_panel = ((panel_term - unit_rows * along_panel[:, None]) * inv_rows[:, None]).astype(
        jnp.bfloat16
    )
    grad_tokens = ((token_term - unit_cols * along_tokens[:, None]) * inv_cols[:, None]).astype(
        jnp.bfloat16
    )
    grad_tokens = lax.all_gather(grad_tokens, "row", axis=0, tiled=True)
    return (row_loss, grad_panel, grad_tokens)


def solution(mesh):
    placed = (P("row", "feat"), P("row", "feat"), P("col", "feat"), P("col", "feat"))
    return jax.shard_map(
        local,
        mesh=mesh,
        in_specs=placed,
        out_specs=(P(("row", "col")), P(("row", "col"), "feat"), P("col", "feat")),
        check_vma=False,
    )
```

profile of v0, /device:TPU:0, one launch (start us, length us, event | category | flops | bytes accessed | tf_op | source)
XLA Modules:
  0.0 300.2 jit_solution(16195987117583442197)
XLA Ops:
  7.2 5.7 %fusion.9 = f32[512,768]{1,0:T(8,128)} fusion(bf16[512,2048]{1,0:T(8,128)(2,1)} %param.5, bf16[768,2048]{1,0:T(8,128)(2,1)} %param.7), kind=kOutput, calls=%fused_computation.26 | convolution fusion | flops 1610612736 | bytes 6815744 | tf_op jit(solution)/shard_map/rd,cd->rc/dot_general | solution.py:15
  12.9 3.0 fusion.8
  15.9 0.0 reduce-scatter.3.cloned.1.call-start
  15.9 2.2 multiply_reduce_fusion.1
  18.2 0.5 fusion.1
  18.7 0.7 multiply_reduce_fusion
  19.4 1.2 copy-done.2
  20.6 0.7 fusion
  21.2 9.9 %all-reduce.2 = (f32[768]{0:T(1024)S(1)}, f32[512]{0:T(512)S(1)}, f32[768]{0:T(1024)S(1)}, f32[512]{0:T(512)S(1)}) all-reduce(f32[768]{0:T(1024)S(1)} %multiply_reduce_fusion, f32[512]{0:T(512)S(1)} %multiply_reduce_fusion.1, f32[768]{0:T(1024)S(1)} %fusion, f32[512]{0:T(512)S(1)} %fusion.1), channel_id=1, replica_groups=mesh['row'=4,'col'=4,'feat'=2] {'feat'}, use_global_device_ids=true, to_apply=%region_9.0 | all-reduce | flops 2560 | bytes 20480 | tf_op jit(solution)/shard_map/psum | solution.py:23
  31.2 73.9 %all-reduce.6.cloned.1.call-done = (f32[512,768]{1,0:T(8,128)}, f32[512,768]{1,0:T(8,128)}) async-done(((f32[512,768]{1,0:T(8,128)}, f32[512,768]{1,0:T(8,128)}), (f32[512,768]{1,0:T(8,128)}, f32[512,768]{1,0:T(8,128)})) %all-reduce.6.cloned.1.call-update) | async-done | bytes 3145744 | tf_op jit(solution)/shard_map/psum | solution.py:23
  105.1 2.6 multiply_reduce_fusion.3
  107.7 1.1 copy-done.6
  108.8 3.9 %fusion.2 = f32[512,2048]{1,0:T(8,128)} fusion(f32[512,768]{1,0:T(8,128)S(1)} %get-tuple-element.12, bf16[768,2048]{1,0:T(8,128)(2,1)S(1)} %copy-done.3, f32[768]{0:T(1024)S(1)} %get-tuple-element.14), kind=kOutput, calls=%fused_computation.8 | convolution fusion | flops 1616117760 | bytes 8915968 | tf_op jit(solution)/shard_map/dot_general | solution.py:47
  112.8 6.0 %fusion.4 = f32[768,2048]{1,0:T(8,128)} fusion(f32[512,768]{1,0:T(8,128)} %copy-done.6, bf16[512,2048]{1,0:T(8,128)(2,1)S(1)} %copy-done, f32[512]{0:T(512)S(1)} %get-tuple-element.16), kind=kOutput, calls=%fused_computation.10 | convolution fusion | flops 1614544896 | bytes 9963520 | tf_op jit(solution)/shard_map/rc,rd->cd/dot_general | solution.py:52
  118.8 0.0 all-gather.2.cloned.1.call-start
  118.8 0.1 dynamic_slice.15
  118.9 2.5 convert_multiply_fusion.2
  121.4 1.1 copy-done.4
  122.5 3.1 %convert_multiply_fusion = f32[768,2048]{1,0:T(8,128)} fusion(bf16[768,2048]{1,0:T(8,128)(2,1)S(1)} %copy-done.4, f32[768]{0:T(1024)S(1)} %get-tuple-element.14), kind=kLoop, calls=%fused_computation | loop fusion | flops 3145728 | bytes 9440256 | tf_op jit(solution)/shard_map/mul | solution.py:44
  125.6 64.0 %reduce-scatter.3.cloned.1.call-done = f32[128,2048]{1,0:T(8,128)} async-done(((f32[512,2048]{1,0:T(8,128)}), f32[128,2048]{1,0:T(8,128)}) %reduce-scatter.3.cloned.1.call-update) | async-done | bytes 1048592 | tf_op jit(solution)/shard_map/reduce_scatter | solution.py:49
  189.6 1.7 multiply_reduce_fusion.4
  191.4 59.7 %reduce-scatter.5.cloned.1.call-done = f32[192,2048]{1,0:T(8,128)} async-done(((f32[768,2048]{1,0:T(8,128)}), f32[192,2048]{1,0:T(8,128)}) %reduce-scatter.5.cloned.1.call-update) | async-done | bytes 1572880 | tf_op jit(solution)/shard_map/reduce_scatter | solution.py:53
  251.1 2.2 multiply_reduce_fusion.2
  253.3 4.9 %all-reduce.1 = (f32[128]{0:T(128)S(1)}, f32[192]{0:T(256)S(1)}) all-reduce(f32[128]{0:T(128)S(1)} %multiply_reduce_fusion.4, f32[192]{0:T(256)S(1)} %multiply_reduce_fusion.2), channel_id=1, replica_groups=mesh['row'=4,'col'=4,'feat'=2] {'feat'}, use_global_device_ids=true, to_apply=%region_14.0 | all-reduce | flops 320 | bytes 2560 | tf_op jit(solution)/shard_map/psum | solution.py:62
  258.2 2.7 multiply_convert_fusion
  261.0 0.1 dynamic_slice.13
  261.1 0.6 dynamic-slice
  262.3 11.7 %all-reduce = f32[512]{0:T(512)S(1)} all-reduce(f32[512]{0:T(512)S(1)} %get-tuple-element.11), channel_id=2, replica_groups=mesh['row'=4,'col'=4,'feat'=2] {'col'}, use_global_device_ids=true, to_apply=%region_11.0.clone | all-reduce | flops 512 | bytes 4096
  274.0 0.6 dynamic-slice.1
  274.6 2.3 multiply_convert_fusion.2
  276.9 12.8 %all-gather.2.cloned.1.call-done = bf16[768,2048]{1,0:T(8,128)(2,1)} async-done(((bf16[192,2048]{1,0:T(8,128)(2,1)}), bf16[768,2048]{1,0:T(8,128)(2,1)}) %all-gather.2.cloned.1.call-update) | async-done | bytes 3145744 | tf_op jit(solution)/shard_map/all_gather | solution.py:71
  289.7 4.0 %copy.10 = bf16[768,2048]{1,0:T(8,128)(2,1)} copy(bf16[768,2048]{1,0:T(8,128)(2,1)} %all-gather.2.cloned.1.call-done) | data formatting | bytes 6291456
  (25 shorter events, 0.2 us)
Async XLA Ops:
  7.2 5.7 %copy-start = (bf16[512,2048]{1,0:T(8,128)(2,1)S(1)}, bf16[512,2048]{1,0:T(8,128)(2,1)}, u32[]{:S(2)}) copy-start(bf16[512,2048]{1,0:T(8,128)(2,1)} %param.4) | copy-start | bytes 6291460
  7.2 97.9 %all-reduce.6.cloned.1.call-start = ((), (), s32[]{:S(2)}) async-start(), calls=%async_computation.5 | async-start | bytes 6291456 | tf_op jit(solution)/shard_map/psum | solution.py:23
  7.2 5.7 %copy-start.1 = (bf16[768,2048]{1,0:T(8,128)(2,1)S(1)}, bf16[768,2048]{1,0:T(8,128)(2,1)}, u32[]{:S(2)}) copy-start(bf16[768,2048]{1,0:T(8,128)(2,1)} %param.6) | copy-start | bytes 9437188
  15.9 173.8 %reduce-scatter.3.cloned.1.call-start = ((), (), s32[]{:S(2)}) async-start(), calls=%async_computation.2 | async-start | bytes 5242880 | tf_op jit(solution)/shard_map/reduce_scatter | solution.py:49
  15.9 2.7 copy-start.8
  18.7 1.9 copy-start.2
  105.1 3.8 %copy-start.3 = (bf16[768,2048]{1,0:T(8,128)(2,1)S(1)}, bf16[768,2048]{1,0:T(8,128)(2,1)}, u32[]{:S(2)}) copy-start(bf16[768,2048]{1,0:T(8,128)(2,1)} %param.6) | copy-start | bytes 9437188
  107.7 1.1 copy-start.6
  112.7 138.4 %reduce-scatter.5.cloned.1.call-start = ((), (), s32[]{:S(2)}) async-start(), calls=%async_computation.3 | async-start | bytes 7864320 | tf_op jit(solution)/shard_map/reduce_scatter | solution.py:53
  118.8 170.9 %all-gather.2.cloned.1.call-start = ((), (), s32[]{:S(2)}) async-start(), calls=%async_computation.4 | async-start | bytes 3932160 | tf_op jit(solution)/shard_map/all_gather | solution.py:71
  118.9 3.6 %copy-start.4 = (bf16[768,2048]{1,0:T(8,128)(2,1)S(1)}, bf16[768,2048]{1,0:T(8,128)(2,1)}, u32[]{:S(2)}) copy-start(bf16[768,2048]{1,0:T(8,128)(2,1)} %param.6) | copy-start | bytes 9437188
  251.1 7.2 %copy-start.5 = (f32[192,2048]{1,0:T(8,128)S(1)}, f32[192,2048]{1,0:T(8,128)}, u32[]{:S(2)}) copy-start(f32[192,2048]{1,0:T(8,128)} %reduce-scatter.5.cloned.1.call-done) | copy-start | bytes 4718596
  258.2 2.8 copy-start.9
  258.2 16.3 %copy-start.7 = (f32[128,2048]{1,0:T(8,128)S(1)}, f32[128,2048]{1,0:T(8,128)}, u32[]{:S(2)}) copy-start(f32[128,2048]{1,0:T(8,128)} %reduce-scatter.3.cloned.1.call-done) | copy-start | bytes 3145732
Sparse Core Ops, SparseCore 0:
  16.0 88.9 all-reduce.5
  112.8 76.7 reduce-scatter.2
  192.2 58.8 reduce-scatter.4
  261.1 28.5 all-gather.1
where the time goes:
time: 301 us; the launch traced here: 300 us
  waiting for transfers between devices  211 us (70%)
  blocking collectives  26.5 us (9%)
  other arithmetic  21.3 us (7%)
  matrix products  18.5 us (6%)
  between operations  14.5 us (5%)
  local copies, waits for them, and re-layouts  8.75 us (3%)
    psum x1, waiting for transfers between devices, local(): lax.psum((inner(panel_student, tokens_student), inner(panel_teacher, toke...  73.9 us
    reduce_scatter x1, waiting for transfers between devices, local(): lax.psum_scatter(panel_part, 'col', scatter_dimension=0, tiled=True)  64 us
    reduce_scatter x1, waiting for transfers between devices, local(): lax.psum_scatter(token_part, 'row', scatter_dimension=0, tiled=True)  59.7 us
    all_gather x1, waiting for transfers between devices, local(): grad_tokens = lax.all_gather(grad_tokens, 'row', axis=0, tiled=True)  12.8 us
    unnamed x1, blocking collectives  11.7 us
    psum x1, blocking collectives, local(): lax.psum((inner(panel_student, tokens_student), inner(panel_teacher, toke...  9.91 us
    dot_general x2, matrix products, inner(): jnp.einsum('rd,cd->rc', left, right, preferred_element_type=jnp.float32)  8.62 us
    unnamed x23, local copies, waits for them, and re-layouts  8.6 us
  transfers between devices with their start and end apart: 4, of which 4 were waited for; matrix products, arithmetic and copies ran while one was open for 7% of the time, Pallas kernels for 0%

commit v1 on v0

v1 whole, which is shorter than its diff:
```python
import functools

import jax
import jax.numpy as jnp
from jax import lax
from jax.experimental import pallas as pl
from jax.experimental.pallas import tpu as pltpu
from jax.sharding import PartitionSpec as P

epsilon = 1e-06
MESH = pl.DeviceIdType.MESH
f32, bf16 = jnp.float32, jnp.bfloat16
LANE = 128
CHUNK = 256


def nt(a, b):
    return lax.dot_general(a, b, (((1,), (1,)), ((), ())), preferred_element_type=f32)


def loop(count, body):
    def step(i, carry):
        body(i)
        return carry

    lax.fori_loop(0, count, step, 0)


def at(i, size):
    return pl.ds(pl.multiple_of(i * size, size), size)


def to_row(acc):
    rows = acc.shape[0]
    if rows < LANE:
        acc = jnp.concatenate([acc, jnp.zeros((LANE - rows, LANE), f32)], axis=0)
    return jnp.sum(acc.T, axis=0, keepdims=True)


def to_column(row):
    return jnp.broadcast_to(row, (LANE, row.shape[1])).T


def kernel(
    rows_n, cols_n,
    ps_h, pt_h, ts_h, tt_h,
    loss_o, gp_o, gt_o,
    ps, pt, ts, tt, ph, th,
    sq, sqr, inv, psc, ptc, tsc,
    m1, g1t, m2, xs1, xr1, xs2, xr2, d_all, dts,
    loss_acc, lsend, lrecv,
    part, zs, zr, zl,
    tpart, cs, cr, ys, yr,
    als, alr,
    lsem, sqsem, x1sem, x2s, x2r, cos, cor, yos, yor, zss, zrr, zlr, los, lor, als_s, alr_s, ags, agr, outs,
):
    N = cols_n
    Pn, F = ps.shape
    T = ts.shape[0]
    C = T // CHUNK
    rp = Pn // N
    nr = Pn - rp
    row, col, feat = lax.axis_index("row"), lax.axis_index("col"), lax.axis_index("feat")
    xdev = {"feat": 1 - feat}
    low = row % 2
    cdev = {"row": row + 1 - 2 * low}
    ydev = {"row": row + 2 - 4 * ((row // 2) % 2)}
    first_half = col < N // 2
    r1 = pl.multiple_of(jnp.where(first_half, N - 1, 0) * rp, rp)
    r2 = pl.multiple_of(jnp.where(first_half, 0, 1) * rp, rp)
    HC = CHUNK // 2

    loads = [
        pltpu.make_async_copy(h, v, lsem.at[i])
        for i, (h, v) in enumerate(((ps_h, ps), (ts_h, ts), (pt_h, pt), (tt_h, tt)))
    ]
    for load in loads:
        load.start()

    barrier = pltpu.get_barrier_semaphore()
    for dev in (xdev, cdev, ydev):
        pl.semaphore_signal(barrier, inc=1, device_id=dev, device_id_type=MESH)
    for k in range(1, N):
        pl.semaphore_signal(barrier, inc=1, device_id={"col": (col + k) % N}, device_id_type=MESH)
    pl.semaphore_wait(barrier, 3 + N - 1)

    def remote(src, dst, s, r, dev):
        return pltpu.make_async_remote_copy(
            src_ref=src, dst_ref=dst, send_sem=s, recv_sem=r, device_id=dev, device_id_type=MESH
        )

    sq[...] = jnp.zeros_like(sq)

    def squares(ref, i, count):
        def body(t):
            acc = jnp.zeros((LANE, LANE), f32)
            for k in range(F // LANE):
                v = ref[at(t, LANE), k * LANE:(k + 1) * LANE].astype(f32)
                acc = acc + v * v
            sq[i:i + 1, at(t, LANE)] = to_row(acc)

        loop(count // LANE, body)

    for load, (ref, i, count) in zip(loads, ((ps, 0, Pn), (ts, 2, T), (pt, 1, Pn), (tt, 3, T))):
        load.wait()
        squares(ref, i, count)
    sq_copy = remote(sq, sqr, sqsem.at[0], sqsem.at[1], xdev)
    sq_copy.start()

    def raw(c):
        m1[c] = nt(ps[pl.ds(r1, rp), :], ts[at(c, CHUNK), :])
        g1t[c] = nt(pt[pl.ds(r1, rp), :], tt[at(c, CHUNK), :])

    loop(C, raw)
    sq_copy.wait_recv()
    inv[...] = 1.0 / jnp.sqrt(sq[...] + sqr[...] + epsilon)
    for i, ref in ((0, psc), (1, ptc), (2, tsc)):
        for t in range(ref.shape[0] // LANE):
            ref[t * LANE:(t + 1) * LANE, :] = to_column(inv[i:i + 1, t * LANE:(t + 1) * LANE])

    def scaled(gs, gt, c, r0, count, m_ref, s_ref):
        for j in range(CHUNK // LANE):
            lanes = slice(j * LANE, (j + 1) * LANE)
            where = pl.ds(pl.multiple_of(c * CHUNK + j * LANE, LANE), LANE)
            m = gs[:, lanes] * psc[pl.ds(r0, count), :] * inv[2:3, where]
            m = m - gt[:, lanes] * ptc[pl.ds(r0, count), :] * inv[3:4, where]
            m_ref[c, :, lanes] = m
            s_ref[c, :, lanes] = m.astype(bf16)

    loop(C, lambda c: scaled(m1[c], g1t[c], c, r1, rp, m1, xs1))
    x1_copy = remote(xs1, xr1, x1sem.at[0], x1sem.at[1], xdev)
    x1_copy.start()

    def x2_copy(c):
        return remote(xs2.at[c], xr2.at[c], x2s.at[c], x2r.at[c], xdev)

    def rest(c):
        gs = nt(ps[pl.ds(r2, nr), :], ts[at(c, CHUNK), :])
        gt = nt(pt[pl.ds(r2, nr), :], tt[at(c, CHUNK), :])
        scaled(gs, gt, c, r2, nr, m2, xs2)
        x2_copy(c).start()

    loop(C, rest)

    def halves(src, column, dst):
        def body(t):
            scale = column[at(t, LANE), :]
            for k in range(F // LANE):
                lanes = slice(k * LANE, (k + 1) * LANE)
                dst[at(t, LANE), lanes] = (src[at(t, LANE), lanes].astype(f32) * scale).astype(bf16)

        loop(src.shape[0] // LANE, body)

    halves(ts, tsc, th)
    halves(ps, psc, ph)

    loss_acc[...] = jnp.zeros_like(loss_acc)

    def settle(m_ref, x_ref, c, r0, count):
        for j in range(CHUNK // LANE):
            lanes = slice(j * LANE, (j + 1) * LANE)
            m = m_ref[c, :, lanes] + x_ref[c, :, lanes].astype(f32)
            where = pl.ds(pl.multiple_of(c * CHUNK + j * LANE, LANE), LANE)
            d_all[pl.ds(r0, count), where] = (2.0 * m).astype(bf16)
            loss_acc[pl.ds(r0, count), :] += m * m

    def panel_product(r0, count):
        def body(n):
            part[pl.ds(r0, count), at(n, CHUNK)] = jnp.dot(
                d_all[pl.ds(r0, count), :], th[:, at(n, CHUNK)], preferred_element_type=f32
            )

        loop(F // CHUNK, body)

    def block(d):
        return pl.ds(pl.multiple_of(d * rp, rp), rp)

    def right(d):
        return remote(zs.at[block(d), :], zr.at[block(d), :], zss.at[d], zrr.at[d], {"col": (col + 1) % N})

    def left(d):
        return remote(zs.at[block(d), :], zl.at[block(d), :], zss.at[d], zlr.at[d], {"col": (col + N - 1) % N})

    def forward(d, copy, arrived):
        def body(n):
            value = part[block(d), at(n, CHUNK)]
            if arrived is not None:
                value = value + arrived[block(d), at(n, CHUNK)].astype(f32)
            zs[block(d), at(n, CHUNK)] = value.astype(bf16)

        if arrived is not None:
            copy(d).wait_recv()
        loop(F // CHUNK, body)
        copy(d).start()

    x1_copy.wait_recv()
    loop(C, lambda c: settle(m1, xr1, c, r1, rp))
    panel_product(r1, rp)

    @pl.when(col == 0)
    def _():
        forward(N - 1, right, None)

    @pl.when(col == N - 1)
    def _():
        forward(0, left, None)

    def core_copy(c):
        return remote(cs.at[c], cr.at[c], cos.at[c], cor.at[c], cdev)

    def y_copy(c):
        return remote(ys.at[c], yr.at[c], yos.at[c], yor.at[c], ydev)

    mine = pl.ds(pl.multiple_of(low * HC, HC), HC)
    other = pl.ds(pl.multiple_of((1 - low) * HC, HC), HC)

    def token_product(c):
        dts[...] = d_all[:, at(c, CHUNK)].T

        def body(n):
            tpart[:, at(n, CHUNK)] = jnp.dot(dts[...], ph[:, at(n, CHUNK)], preferred_element_type=f32)
            cs[c, :, at(n, CHUNK)] = tpart[other, at(n, CHUNK)].astype(bf16)

        loop(F // CHUNK, body)
        core_copy(c).start()
        core_copy(c).wait_recv()

        def add(n):
            value = tpart[mine, at(n, CHUNK)] + cr[c, :, at(n, CHUNK)].astype(f32)
            ys[c, :, at(n, CHUNK)] = value.astype(bf16)

        loop(F // CHUNK, add)
        y_copy(c).start()

    def arrive(c):
        x2_copy(c).wait_recv()
        settle(m2, xr2, c, r2, nr)

    def both(c):
        arrive(c)
        token_product(c)

    loop(C - 1, both)
    arrive(C - 1)
    panel_product(r2, nr)

    @pl.when(col == 0)
    def _():
        for d in range(N - 2, 0, -1):
            forward(d, right, None)

    @pl.when(col == N - 1)
    def _():
        for d in range(1, N - 1):
            forward(d, left, None)

    @pl.when((col > 0) & (col < N // 2))
    def _():
        forward(N - 1, right, zr)

    @pl.when((col < N - 1) & (col >= N // 2))
    def _():
        forward(0, left, zl)

    token_product(C - 1)

    def loss_copy(d, src):
        return remote(lsend.at[d], lrecv.at[src], los.at[d], lor.at[src], {"col": d})

    def loss_rows(d):
        lsend[d] = jnp.broadcast_to(to_row(loss_acc[block(d), :]), lsend.shape[1:])

    loop(N, loss_rows)
    for k in range(1, N):
        d = (col + k) % N
        loss_copy(d, col).start()

    def along_copy(i):
        return remote(als.at[i], alr.at[i], als_s.at[i], alr_s.at[i], xdev)

    def token_rows(c):
        return pl.ds(pl.multiple_of(c * CHUNK + low * HC, HC), HC)

    def token_term(c, lanes):
        return ys[c, :, lanes].astype(f32) + yr[c, :, lanes].astype(f32)

    def token_along(c):
        y_copy(c).wait_recv()
        scale = tsc[token_rows(c), :]
        acc = jnp.zeros((HC, LANE), f32)
        for k in range(F // LANE):
            lanes = slice(k * LANE, (k + 1) * LANE)
            acc = acc + ts[token_rows(c), lanes].astype(f32) * scale * token_term(c, lanes)
        als[c] = jnp.broadcast_to(to_row(acc), als.shape[1:])
        along_copy(c).start()

    def gather_copy(c):
        return remote(cr.at[c], gt_o.at[token_rows(c), :], ags.at[c], agr.at[c], cdev)

    def own_copy(c):
        return pltpu.make_async_copy(cr.at[c], gt_o.at[token_rows(c), :], outs.at[c])

    def token_finish(c):
        along_copy(c).wait_recv()
        along = to_column(als[c, 0:1, :] + alr[c, 0:1, :])
        scale = tsc[token_rows(c), :]
        for k in range(F // LANE):
            lanes = slice(k * LANE, (k + 1) * LANE)
            unit = ts[token_rows(c), lanes].astype(f32) * scale
            cr[c, :, lanes] = ((token_term(c, lanes) - unit * along) * scale).astype(bf16)
        gather_copy(c).start()
        own_copy(c).start()

    def chain(k):
        d = N - 1 - k
        go = (col < d) & (col > 0)
        if k == 0:
            go = go & (col >= N // 2)

        @pl.when(go)
        def _():
            forward(d, right, zr)

        e = k
        go = (col > e) & (col < N - 1)
        if k == 0:
            go = go & (col < N // 2)

        @pl.when(go)
        def _():
            forward(e, left, zl)

    for i in range(max(C, N - 1)):
        if i < N - 1:
            chain(i)
        if i < C:
            token_along(i)
        if 0 < i < C:
            token_finish(i - 1)

    own = block(col)

    def absorb(arrived):
        def body(n):
            part[own, at(n, CHUNK)] += arrived[own, at(n, CHUNK)].astype(f32)

        loop(F // CHUNK, body)

    @pl.when(col > 0)
    def _():
        right(col).wait_recv()
        absorb(zr)

    @pl.when(col < N - 1)
    def _():
        left(col).wait_recv()
        absorb(zl)

    scale = psc[own, :]
    acc = jnp.zeros((rp, LANE), f32)
    for k in range(F // LANE):
        lanes = slice(k * LANE, (k + 1) * LANE)
        acc = acc + ps[own, lanes].astype(f32) * scale * part[own, lanes]
    als[C] = jnp.broadcast_to(to_row(acc), als.shape[1:])
    along_copy(C).start()
    token_finish(C - 1)
    total = lsend[col]
    for k in range(1, N):
        src = (col + N - k) % N
        loss_copy(col, src).wait_recv()
        total = total + lrecv[src]
    loss_o[...] = total
    along_copy(C).wait_recv()
    along = to_column(als[C, 0:1, :] + alr[C, 0:1, :])[:rp]
    for k in range(F // LANE):
        lanes = slice(k * LANE, (k + 1) * LANE)
        unit = ps[own, lanes].astype(f32) * scale
        gp_o[:, lanes] = ((part[own, lanes] - unit * along) * scale).astype(bf16)

    sq_copy.wait_send()
    x1_copy.wait_send()

    def ends(c):
        x2_copy(c).wait_send()
        core_copy(c).wait_send()
        y_copy(c).wait_send()
        along_copy(c).wait_send()
        gather_copy(c).wait_send()
        gather_copy(c).wait_recv()
        own_copy(c).wait()

    loop(C, ends)
    along_copy(C).wait_send()

    for k in range(1, N):
        d = (col + k) % N
        loss_copy(d, col).wait_send()
        right(d).wait_send()


def local(rows_n, cols_n, panel_student, panel_teacher, tokens_student, tokens_teacher):
    Pn, F = panel_student.shape
    T = tokens_student.shape[0]
    N, C = cols_n, T // CHUNK
    rp = Pn // N
    nr, HC, W = Pn - rp, CHUNK // 2, max(Pn, T)
    lp = max(rp, LANE)
    V, S = pltpu.VMEM, pltpu.SemaphoreType.DMA
    scratch = [
        V((Pn, F), bf16), V((Pn, F), bf16), V((T, F), bf16), V((T, F), bf16), V((Pn, F), bf16), V((T, F), bf16),
        V((8, W), f32), V((8, W), f32), V((8, W), f32), V((Pn, LANE), f32), V((Pn, LANE), f32), V((T, LANE), f32),
        V((C, rp, CHUNK), f32), V((C, rp, CHUNK), f32), V((C, nr, CHUNK), f32),
        V((C, rp, CHUNK), bf16), V((C, rp, CHUNK), bf16), V((C, nr, CHUNK), bf16), V((C, nr, CHUNK), bf16),
        V((Pn, T), bf16), V((CHUNK, Pn), bf16),
        V((Pn, LANE), f32), V((N, 8, lp), f32), V((N, 8, lp), f32),
        V((Pn, F), f32), V((Pn, F), bf16), V((Pn, F), bf16), V((Pn, F), bf16),
        V((CHUNK, F), f32), V((C, HC, F), bf16), V((C, HC, F), bf16), V((C, HC, F), bf16), V((C, HC, F), bf16),
        V((C + 1, 8, lp), f32), V((C + 1, 8, lp), f32),
        S((4,)), S((2,)), S((2,)), S((C,)), S((C,)), S((C,)), S((C,)), S((C,)), S((C,)),
        S((N,)), S((N,)), S((N,)), S((N,)), S((N,)), S((C + 1,)), S((C + 1,)), S((C,)), S((C,)), S((C,)),
    ]
    anywhere, vmem = pl.BlockSpec(memory_space=pl.ANY), pl.BlockSpec(memory_space=pltpu.VMEM)
    loss, grad_panel, grad_tokens = pl.pallas_call(
        functools.partial(kernel, rows_n, cols_n),
        out_shape=(
            jax.ShapeDtypeStruct((8, lp), f32),
            jax.ShapeDtypeStruct((rp, F), bf16),
            jax.ShapeDtypeStruct((T, F), bf16),
        ),
        in_specs=[anywhere] * 4,
        out_specs=(vmem, vmem, anywhere),
        scratch_shapes=scratch,
        compiler_params=pltpu.CompilerParams(
            collective_id=0, has_side_effects=True, vmem_limit_bytes=62 * 1024 * 1024
        ),
    )(panel_student, panel_teacher, tokens_student, tokens_teacher)
    return loss[0, :rp], grad_panel, grad_tokens


def solution(mesh):
    placed = (P("row", "feat"), P("row", "feat"), P("col", "feat"), P("col", "feat"))
    return jax.shard_map(
        functools.partial(local, mesh.shape["row"], mesh.shape["col"]),
        mesh=mesh,
        in_specs=placed,
        out_specs=(P(("row", "col")), P(("row", "col"), "feat"), P("col", "feat")),
        check_vma=False,
    )
```

time: 301 us -> 76 us (0.25)
  waiting for transfers between devices: 211 us -> 0 us
  Pallas kernels: 0 us -> 68.1 us
  blocking collectives: 26.5 us -> 0 us
  other arithmetic: 21.3 us -> 0 us
  matrix products: 18.5 us -> 0 us
  between operations: 14.5 us -> 0.64 us
    reduce_scatter x2 -> x0, waiting for transfers between devices: 124 us -> none  [the longest x1 64 us: local(): lax.psum_scatter(panel_part, 'col', scatter_dimension=0, tiled=True)]
    psum x1 -> x0, waiting for transfers between devices: 73.9 us -> none  [local(): lax.psum((inner(panel_student, tokens_student), inner(panel_teacher, toke...]
    pallas_call x0 -> x1, Pallas kernels: none -> 68.1 us  [local(): pl.pallas_call(functools.partial(kernel, rows_n, cols_n), out_shape=(jax....]
    dot_general x4 -> x0, matrix products: 18.5 us -> none  [the longest x2 8.62 us: inner(): jnp.einsum('rd,cd->rc', left, right, preferred_element_type=jnp.float32)]
    psum x2 -> x0, blocking collectives: 14.8 us -> none  [the longest x1 9.91 us: local(): lax.psum((inner(panel_student, tokens_student), inner(panel_teacher, toke...]
    all_gather x1 -> x0, waiting for transfers between devices: 12.8 us -> none  [local(): grad_tokens = lax.all_gather(grad_tokens, 'row', axis=0, tiled=True)]
    unnamed x1 -> x0, blocking collectives: 11.7 us -> none
    reduce_sum x7 -> x0, other arithmetic: 10.6 us -> none  [the longest x4 4.07 us: squares(): return jnp.sum(values * values, axis=1)]
  transfers between devices with their start and end apart: 4 -> 0, of which waited for: 4 -> 0; matrix products, arithmetic and copies ran while one was open for 7% -> 0% of each run, Pallas kernels for 0% -> 0%
where the time goes in v1:
time: 76 us; the launch traced here: 75.8 us
  Pallas kernels  68.1 us (90%)
  local copies, waits for them, and re-layouts  7.04 us (9%)
    pallas_call x1, Pallas kernels, local(): pl.pallas_call(functools.partial(kernel, rows_n, cols_n), out_shape=(jax....  68.1 us
    unnamed x2, local copies, waits for them, and re-layouts  5.85 us

profile of v1, /device:TPU:0, one launch (start us, length us, event | category | flops | bytes accessed | tf_op | source)
XLA Modules:
  0.0 75.8 jit_solution(10850595987685615706)
XLA Ops:
  0.6 68.1 %shard_map.67 = (f32[8,128]{1,0:T(8,128)}, bf16[128,2048]{1,0:T(8,128)(2,1)}, bf16[768,2048]{1,0:T(8,128)(2,1)}) custom-call(bf16[512,2048]{1,0:T(8,128)(2,1)} %ps_h.1, bf16[512,2048]{1,0:T(8,128)(2,1)} %pt_h.1, bf16[768,2048]{1,0:T(8,128)(2,1)} %ts_h.1, bf16[768,2048]{1,0:T(8,128)(2,1)} %tt_h.1), custom_call_target="tpu_custom_call" | custom-call | tf_op jit(solution)/shard_map/pallas_call | solution.py:423
  68.7 1.2 %slice_bitcast_fusion = f32[128]{0:T(128)} fusion(f32[8,128]{1,0:T(8,128)} %get-tuple-element.6), kind=kLoop, calls=%fused_computation | loop fusion | bytes 1024 | tf_op jit(solution)/shard_map/squeeze | solution.py:437
  69.9 1.9 %copy.9 = bf16[128,2048]{1,0:T(8,128)(2,1)} copy(bf16[128,2048]{1,0:T(8,128)(2,1)} %get-tuple-element.13) | data formatting | bytes 1048576
  71.8 4.0 %copy.10 = bf16[768,2048]{1,0:T(8,128)(2,1)} copy(bf16[768,2048]{1,0:T(8,128)(2,1)} %get-tuple-element.14) | data formatting | bytes 6291456

commit v2 on v1

--- a/solution.py
+++ b/solution.py
@@ -12,6 +12,7 @@
 f32, bf16 = jnp.float32, jnp.bfloat16
 LANE = 128
 CHUNK = 256
+TILE = 1024
 
 
 def nt(a, b):
@@ -47,7 +48,7 @@
     loss_o, gp_o, gt_o,
     ps, pt, ts, tt, ph, th,
     sq, sqr, inv, psc, ptc, tsc,
-    m1, g1t, m2, xs1, xr1, xs2, xr2, d_all, dts,
+    m1, g1t, g2t, m2, xs1, xr1, xs2, xr2, d_all, dts,
     loss_acc, lsend, lrecv,
     part, zs, zr, zl,
     tpart, cs, cr, ys, yr,
@@ -64,7 +65,9 @@
     xdev = {"feat": 1 - feat}
     low = row % 2
     cdev = {"row": row + 1 - 2 * low}
-    ydev = {"row": row + 2 - 4 * ((row // 2) % 2)}
+    across = row + 2 - 4 * ((row // 2) % 2)
+    ydev = {"row": across}
+    xydev = {"row": across, "feat": 1 - feat}
     first_half = col < N // 2
     r1 = pl.multiple_of(jnp.where(first_half, N - 1, 0) * rp, rp)
     r2 = pl.multiple_of(jnp.where(first_half, 0, 1) * rp, rp)
@@ -78,11 +81,11 @@
         load.start()
 
     barrier = pltpu.get_barrier_semaphore()
-    for dev in (xdev, cdev, ydev):
+    for dev in (xdev, cdev, ydev, xydev):
         pl.semaphore_signal(barrier, inc=1, device_id=dev, device_id_type=MESH)
     for k in range(1, N):
         pl.semaphore_signal(barrier, inc=1, device_id={"col": (col + k) % N}, device_id_type=MESH)
-    pl.semaphore_wait(barrier, 3 + N - 1)
+    pl.semaphore_wait(barrier, 4 + N - 1)
 
     def remote(src, dst, s, r, dev):
         return pltpu.make_async_remote_copy(
@@ -107,11 +110,11 @@
     sq_copy = remote(sq, sqr, sqsem.at[0], sqsem.at[1], xdev)
     sq_copy.start()
 
-    def raw(c):
-        m1[c] = nt(ps[pl.ds(r1, rp), :], ts[at(c, CHUNK), :])
-        g1t[c] = nt(pt[pl.ds(r1, rp), :], tt[at(c, CHUNK), :])
-
-    loop(C, raw)
+    first = slice(0, CHUNK)
+    m1[0] = nt(ps[pl.ds(r1, rp), :], ts[first, :])
+    m2[0] = nt(ps[pl.ds(r2, nr), :], ts[first, :])
+    g1t[...] = nt(pt[pl.ds(r1, rp), :], tt[first, :])
+    g2t[...] = nt(pt[pl.ds(r2, nr), :], tt[first, :])
     sq_copy.wait_recv()
     inv[...] = 1.0 / jnp.sqrt(sq[...] + sqr[...] + epsilon)
     for i, ref in ((0, psc), (1, ptc), (2, tsc)):
@@ -127,20 +130,35 @@
             m_ref[c, :, lanes] = m
             s_ref[c, :, lanes] = m.astype(bf16)
 
-    loop(C, lambda c: scaled(m1[c], g1t[c], c, r1, rp, m1, xs1))
-    x1_copy = remote(xs1, xr1, x1sem.at[0], x1sem.at[1], xdev)
-    x1_copy.start()
-
     def x2_copy(c):
         return remote(xs2.at[c], xr2.at[c], x2s.at[c], x2r.at[c], xdev)
 
-    def rest(c):
+    x0_copy = remote(xs1.at[0], xr1.at[0], x1sem.at[2], x1sem.at[3], xdev)
+    later = pl.ds(1, C - 1)
+    x1_copy = remote(xs1.at[later], xr1.at[later], x1sem.at[0], x1sem.at[1], xdev)
+
+    scaled(m2[0], g2t[...], 0, r2, nr, m2, xs2)
+    x2_copy(0).start()
+    scaled(m1[0], g1t[...], 0, r1, rp, m1, xs1)
+    x0_copy.start()
+
+    def top(i):
+        c = i + 1
+        gs = nt(ps[pl.ds(r1, rp), :], ts[at(c, CHUNK), :])
+        gt = nt(pt[pl.ds(r1, rp), :], tt[at(c, CHUNK), :])
+        scaled(gs, gt, c, r1, rp, m1, xs1)
+
+    loop(C - 1, top)
+    x1_copy.start()
+
+    def rest(i):
+        c = i + 1
         gs = nt(ps[pl.ds(r2, nr), :], ts[at(c, CHUNK), :])
         gt = nt(pt[pl.ds(r2, nr), :], tt[at(c, CHUNK), :])
         scaled(gs, gt, c, r2, nr, m2, xs2)
         x2_copy(c).start()
 
-    loop(C, rest)
+    loop(C - 1, rest)
 
     def halves(src, column, dst):
         def body(t):
@@ -166,11 +184,11 @@
 
     def panel_product(r0, count):
         def body(n):
-            part[pl.ds(r0, count), at(n, CHUNK)] = jnp.dot(
-                d_all[pl.ds(r0, count), :], th[:, at(n, CHUNK)], preferred_element_type=f32
+            part[pl.ds(r0, count), at(n, TILE)] = jnp.dot(
+                d_all[pl.ds(r0, count), :], th[:, at(n, TILE)], preferred_element_type=f32
             )
 
-        loop(F // CHUNK, body)
+        loop(F // TILE, body)
 
     def block(d):
         return pl.ds(pl.multiple_of(d * rp, rp), rp)
@@ -193,18 +211,6 @@
         loop(F // CHUNK, body)
         copy(d).start()
 
-    x1_copy.wait_recv()
-    loop(C, lambda c: settle(m1, xr1, c, r1, rp))
-    panel_product(r1, rp)
-
-    @pl.when(col == 0)
-    def _():
-        forward(N - 1, right, None)
-
-    @pl.when(col == N - 1)
-    def _():
-        forward(0, left, None)
-
     def core_copy(c):
         return remote(cs.at[c], cr.at[c], cos.at[c], cor.at[c], cdev)
 
@@ -214,14 +220,20 @@
     mine = pl.ds(pl.multiple_of(low * HC, HC), HC)
     other = pl.ds(pl.multiple_of((1 - low) * HC, HC), HC)
 
+    def along_copy(c, i):
+        return remote(als.at[c], alr.at[c, i], als_s.at[c, i], alr_s.at[c, i], (xdev, ydev, xydev)[i])
+
+    def token_rows(c):
+        return pl.ds(pl.multiple_of(c * CHUNK + low * HC, HC), HC)
+
     def token_product(c):
         dts[...] = d_all[:, at(c, CHUNK)].T
 
         def body(n):
-            tpart[:, at(n, CHUNK)] = jnp.dot(dts[...], ph[:, at(n, CHUNK)], preferred_element_type=f32)
-            cs[c, :, at(n, CHUNK)] = tpart[other, at(n, CHUNK)].astype(bf16)
-
-        loop(F // CHUNK, body)
+            tpart[:, at(n, TILE)] = jnp.dot(dts[...], ph[:, at(n, TILE)], preferred_element_type=f32)
+            cs[c, :, at(n, TILE)] = tpart[other, at(n, TILE)].astype(bf16)
+
+        loop(F // TILE, body)
         core_copy(c).start()
         core_copy(c).wait_recv()
 
@@ -231,6 +243,14 @@
 
         loop(F // CHUNK, add)
         y_copy(c).start()
+        scale = tsc[token_rows(c), :]
+        acc = jnp.zeros((HC, LANE), f32)
+        for k in range(F // LANE):
+            lanes = slice(k * LANE, (k + 1) * LANE)
+            acc = acc + ts[token_rows(c), lanes].astype(f32) * scale * ys[c, :, lanes].astype(f32)
+        als[c] = jnp.broadcast_to(to_row(acc), als.shape[1:])
+        for i in range(3):
+            along_copy(c, i).start()
 
     def arrive(c):
         x2_copy(c).wait_recv()
@@ -240,7 +260,22 @@
         arrive(c)
         token_product(c)
 
-    loop(C - 1, both)
+    x0_copy.wait_recv()
+    settle(m1, xr1, 0, r1, rp)
+    both(0)
+    x1_copy.wait_recv()
+    loop(C - 1, lambda i: settle(m1, xr1, i + 1, r1, rp))
+    panel_product(r1, rp)
+
+    @pl.when(col == 0)
+    def _():
+        forward(N - 1, right, None)
+
+    @pl.when(col == N - 1)
+    def _():
+        forward(0, left, None)
+
+    loop(C - 2, lambda i: both(i + 1))
     arrive(C - 1)
     panel_product(r2, nr)
 
@@ -268,32 +303,25 @@
         return remote(lsend.at[d], lrecv.at[src], los.at[d], lor.at[src], {"col": d})
 
     def loss_rows(d):
-        lsend[d] = jnp.broadcast_to(to_row(loss_acc[block(d), :]), lsend.shape[1:])
+        rows = block(d)
+        scale = psc[rows, :]
+        acc = jnp.zeros((rp, LANE), f32)
+        for k in range(F // LANE):
+            lanes = slice(k * LANE, (k + 1) * LANE)
+            acc = acc + ps[rows, lanes].astype(f32) * scale * part[rows, lanes]
+        loss_row = to_row(loss_acc[rows, :])
+        along_row = to_row(acc)
+        lsend[d, 0:4, :] = jnp.broadcast_to(loss_row, (4, loss_row.shape[1]))
+        lsend[d, 4:8, :] = jnp.broadcast_to(along_row, (4, along_row.shape[1]))
 
     loop(N, loss_rows)
     for k in range(1, N):
         d = (col + k) % N
         loss_copy(d, col).start()
 
-    def along_copy(i):
-        return remote(als.at[i], alr.at[i], als_s.at[i], alr_s.at[i], xdev)
-
-    def token_rows(c):
-        return pl.ds(pl.multiple_of(c * CHUNK + low * HC, HC), HC)
-
     def token_term(c, lanes):
         return ys[c, :, lanes].astype(f32) + yr[c, :, lanes].astype(f32)
 
-    def token_along(c):
-        y_copy(c).wait_recv()
-        scale = tsc[token_rows(c), :]
-        acc = jnp.zeros((HC, LANE), f32)
-        for k in range(F // LANE):
-            lanes = slice(k * LANE, (k + 1) * LANE)
-            acc = acc + ts[token_rows(c), lanes].astype(f32) * scale * token_term(c, lanes)
-        als[c] = jnp.broadcast_to(to_row(acc), als.shape[1:])
-        along_copy(c).start()
-
     def gather_copy(c):
         return remote(cr.at[c], gt_o.at[token_rows(c), :], ags.at[c], agr.at[c], cdev)
 
@@ -301,8 +329,12 @@
         return pltpu.make_async_copy(cr.at[c], gt_o.at[token_rows(c), :], outs.at[c])
 
     def token_finish(c):
-        along_copy(c).wait_recv()
-        along = to_column(als[c, 0:1, :] + alr[c, 0:1, :])
+        y_copy(c).wait_recv()
+        for i in range(3):
+            along_copy(c, i).wait_recv()
+        here = als[c, 0:1, :] + alr[c, 1, 0:1, :]
+        there = alr[c, 0, 0:1, :] + alr[c, 2, 0:1, :]
+        along = to_column(here + there)
         scale = tsc[token_rows(c), :]
         for k in range(F // LANE):
             lanes = slice(k * LANE, (k + 1) * LANE)
@@ -333,10 +365,17 @@
     for i in range(max(C, N - 1)):
         if i < N - 1:
             chain(i)
+        if i == 0:
+            total = lsend[col]
+            for k in range(1, N):
+                src = (col + N - k) % N
+                loss_copy(col, src).wait_recv()
+                total = total + lrecv[src]
+            loss_o[...] = total
+            als[C] = total
+            along_copy(C, 0).start()
         if i < C:
-            token_along(i)
-        if 0 < i < C:
-            token_finish(i - 1)
+            token_finish(i)
 
     own = block(col)
 
@@ -357,21 +396,8 @@
         absorb(zl)
 
     scale = psc[own, :]
-    acc = jnp.zeros((rp, LANE), f32)
-    for k in range(F // LANE):
-        lanes = slice(k * LANE, (k + 1) * LANE)
-        acc = acc + ps[own, lanes].astype(f32) * scale * part[own, lanes]
-    als[C] = jnp.broadcast_to(to_row(acc), als.shape[1:])
-    along_copy(C).start()
-    token_finish(C - 1)
-    total = lsend[col]
-    for k in range(1, N):
-        src = (col + N - k) % N
-        loss_copy(col, src).wait_recv()
-        total = total + lrecv[src]
-    loss_o[...] = total
-    along_copy(C).wait_recv()
-    along = to_column(als[C, 0:1, :] + alr[C, 0:1, :])[:rp]
+    along_copy(C, 0).wait_recv()
+    along = to_column(als[C, 4:5, :] + alr[C, 0, 4:5, :])[:rp]
     for k in range(F // LANE):
         lanes = slice(k * LANE, (k + 1) * LANE)
         unit = ps[own, lanes].astype(f32) * scale
@@ -379,23 +405,42 @@
 
     sq_copy.wait_send()
     x1_copy.wait_send()
+    x0_copy.wait_send()
 
     def ends(c):
         x2_copy(c).wait_send()
         core_copy(c).wait_send()
         y_copy(c).wait_send()
-        along_copy(c).wait_send()
+        for i in range(3):
+            along_copy(c, i).wait_send()
         gather_copy(c).wait_send()
         gather_copy(c).wait_recv()
         own_copy(c).wait()
 
     loop(C, ends)
-    along_copy(C).wait_send()
+    along_copy(C, 0).wait_send()
 
     for k in range(1, N):
         d = (col + k) % N
         loss_copy(d, col).wait_send()
         right(d).wait_send()
+
+
+def hand_over(loss, panel, tokens, loss_o, panel_o, tokens_o, panel_v, tokens_v, sem_in, sem_out):
+    loss_o[...] = loss[0, :loss_o.shape[0]]
+    moves = [(panel, panel_v, panel_o)]
+    for t in range(0, tokens.shape[0], CHUNK):
+        rows = pl.ds(t, CHUNK)
+        moves.append((tokens.at[rows, :], tokens_v.at[rows, :], tokens_o.at[rows, :]))
+    ins = [pltpu.make_async_copy(a, b, sem_in.at[i]) for i, (a, b, _) in enumerate(moves)]
+    outs = [pltpu.make_async_copy(b, c, sem_out.at[i]) for i, (_, b, c) in enumerate(moves)]
+    for copy in ins:
+        copy.start()
+    for copy, out in zip(ins, outs):
+        copy.wait()
+        out.start()
+    for out in outs:
+        out.wait()
 
 
 def local(rows_n, cols_n, panel_student, panel_teacher, tokens_student, tokens_teacher):
@@ -409,15 +454,15 @@
     scratch = [
         V((Pn, F), bf16), V((Pn, F), bf16), V((T, F), bf16), V((T, F), bf16), V((Pn, F), bf16), V((T, F), bf16),
         V((8, W), f32), V((8, W), f32), V((8, W), f32), V((Pn, LANE), f32), V((Pn, LANE), f32), V((T, LANE), f32),
-        V((C, rp, CHUNK), f32), V((C, rp, CHUNK), f32), V((C, nr, CHUNK), f32),
+        V((C, rp, CHUNK), f32), V((rp, CHUNK), f32), V((nr, CHUNK), f32), V((C, nr, CHUNK), f32),
         V((C, rp, CHUNK), bf16), V((C, rp, CHUNK), bf16), V((C, nr, CHUNK), bf16), V((C, nr, CHUNK), bf16),
         V((Pn, T), bf16), V((CHUNK, Pn), bf16),
         V((Pn, LANE), f32), V((N, 8, lp), f32), V((N, 8, lp), f32),
         V((Pn, F), f32), V((Pn, F), bf16), V((Pn, F), bf16), V((Pn, F), bf16),
         V((CHUNK, F), f32), V((C, HC, F), bf16), V((C, HC, F), bf16), V((C, HC, F), bf16), V((C, HC, F), bf16),
-        V((C + 1, 8, lp), f32), V((C + 1, 8, lp), f32),
-        S((4,)), S((2,)), S((2,)), S((C,)), S((C,)), S((C,)), S((C,)), S((C,)), S((C,)),
-        S((N,)), S((N,)), S((N,)), S((N,)), S((N,)), S((C + 1,)), S((C + 1,)), S((C,)), S((C,)), S((C,)),
+        V((C + 1, 8, lp), f32), V((C + 1, 3, 8, lp), f32),
+        S((4,)), S((2,)), S((4,)), S((C,)), S((C,)), S((C,)), S((C,)), S((C,)), S((C,)),
+        S((N,)), S((N,)), S((N,)), S((N,)), S((N,)), S((C + 1, 3)), S((C + 1, 3)), S((C,)), S((C,)), S((C,)),
     ]
     anywhere, vmem = pl.BlockSpec(memory_space=pl.ANY), pl.BlockSpec(memory_space=pltpu.VMEM)
     loss, grad_panel, grad_tokens = pl.pallas_call(
@@ -434,7 +479,18 @@
             collective_id=0, has_side_effects=True, vmem_limit_bytes=62 * 1024 * 1024
         ),
     )(panel_student, panel_teacher, tokens_student, tokens_teacher)
-    return loss[0, :rp], grad_panel, grad_tokens
+    pieces = T // CHUNK + 1
+    return pl.pallas_call(
+        hand_over,
+        out_shape=(
+            jax.ShapeDtypeStruct((rp,), f32),
+            jax.ShapeDtypeStruct((rp, F), bf16),
+            jax.ShapeDtypeStruct((T, F), bf16),
+        ),
+        in_specs=[vmem, anywhere, anywhere],
+        out_specs=(vmem, anywhere, anywhere),
+        scratch_shapes=[V((rp, F), bf16), V((T, F), bf16), S((pieces,)), S((pieces,))],
+    )(loss, grad_panel, grad_tokens)
 
 
 def solution(mesh):

time: 76 us -> 80.2 us (1.055)
  the two profiles are of different devices: /device:TPU:0 before, /device:TPU:8 now
where the time goes in v2:
time: 80.2 us; the launch traced here: 80 us
  Pallas kernels  79.3 us (99%)
    pallas_call x1, Pallas kernels, local(): pl.pallas_call(functools.partial(kernel, rows_n, cols_n), out_shape=(jax....  75 us
    pallas_call x1, Pallas kernels, local(): pl.pallas_call(hand_over, out_shape=(jax.ShapeDtypeStruct((rp,), f32), ja...  4.37 us

profile of v2, /device:TPU:8, one launch (start us, length us, event | category | flops | bytes accessed | tf_op | source)
XLA Modules:
  0.0 80.0 jit_solution(7430550755840409284)
XLA Ops:
  0.6 75.0 %shard_map.67 = (f32[8,128]{1,0:T(8,128)}, bf16[128,2048]{1,0:T(8,128)(2,1)}, bf16[768,2048]{1,0:T(8,128)(2,1)}) custom-call(bf16[512,2048]{1,0:T(8,128)(2,1)} %ps_h.1, bf16[512,2048]{1,0:T(8,128)(2,1)} %pt_h.1, bf16[768,2048]{1,0:T(8,128)(2,1)} %ts_h.1, bf16[768,2048]{1,0:T(8,128)(2,1)} %tt_h.1), custom_call_target="tpu_custom_call" | custom-call | tf_op jit(solution)/shard_map/pallas_call | solution.py:468
  75.6 4.4 %shard_map.68 = (f32[128]{0:T(128)}, bf16[128,2048]{1,0:T(8,128)(2,1)}, bf16[768,2048]{1,0:T(8,128)(2,1)}) custom-call(f32[8,128]{1,0:T(8,128)} %get-tuple-element.6.loss, bf16[128,2048]{1,0:T(8,128)(2,1)} %get-tuple-element.7.panel, bf16[768,2048]{1,0:T(8,128)(2,1)} %get-tuple-element.8.tokens), custom_call_target="tpu_custom_call" | custom-call | tf_op jit(solution)/shard_map/pallas_call | solution.py:483

commit v3 on v1

--- a/solution.py
+++ b/solution.py
@@ -12,6 +12,7 @@
 f32, bf16 = jnp.float32, jnp.bfloat16
 LANE = 128
 CHUNK = 256
+TILE = 1024
 
 
 def nt(a, b):
@@ -166,11 +167,11 @@
 
     def panel_product(r0, count):
         def body(n):
-            part[pl.ds(r0, count), at(n, CHUNK)] = jnp.dot(
-                d_all[pl.ds(r0, count), :], th[:, at(n, CHUNK)], preferred_element_type=f32
+            part[pl.ds(r0, count), at(n, TILE)] = jnp.dot(
+                d_all[pl.ds(r0, count), :], th[:, at(n, TILE)], preferred_element_type=f32
             )
 
-        loop(F // CHUNK, body)
+        loop(F // TILE, body)
 
     def block(d):
         return pl.ds(pl.multiple_of(d * rp, rp), rp)
@@ -218,10 +219,10 @@
         dts[...] = d_all[:, at(c, CHUNK)].T
 
         def body(n):
-            tpart[:, at(n, CHUNK)] = jnp.dot(dts[...], ph[:, at(n, CHUNK)], preferred_element_type=f32)
-            cs[c, :, at(n, CHUNK)] = tpart[other, at(n, CHUNK)].astype(bf16)
-
-        loop(F // CHUNK, body)
+            tpart[:, at(n, TILE)] = jnp.dot(dts[...], ph[:, at(n, TILE)], preferred_element_type=f32)
+            cs[c, :, at(n, TILE)] = tpart[other, at(n, TILE)].astype(bf16)
+
+        loop(F // TILE, body)
         core_copy(c).start()
         core_copy(c).wait_recv()
 
@@ -396,6 +397,23 @@
         d = (col + k) % N
         loss_copy(d, col).wait_send()
         right(d).wait_send()
+
+
+def hand_over(loss, panel, tokens, loss_o, panel_o, tokens_o, panel_v, tokens_v, sem_in, sem_out):
+    loss_o[...] = loss[0, :loss_o.shape[0]]
+    moves = [(panel, panel_v, panel_o)]
+    for t in range(0, tokens.shape[0], CHUNK):
+        rows = pl.ds(t, CHUNK)
+        moves.append((tokens.at[rows, :], tokens_v.at[rows, :], tokens_o.at[rows, :]))
+    ins = [pltpu.make_async_copy(a, b, sem_in.at[i]) for i, (a, b, _) in enumerate(moves)]
+    outs = [pltpu.make_async_copy(b, c, sem_out.at[i]) for i, (_, b, c) in enumerate(moves)]
+    for copy in ins:
+        copy.start()
+    for copy, out in zip(ins, outs):
+        copy.wait()
+        out.start()
+    for out in outs:
+        out.wait()
 
 
 def local(rows_n, cols_n, panel_student, panel_teacher, tokens_student, tokens_teacher):
@@ -434,7 +452,18 @@
             collective_id=0, has_side_effects=True, vmem_limit_bytes=62 * 1024 * 1024
         ),
     )(panel_student, panel_teacher, tokens_student, tokens_teacher)
-    return loss[0, :rp], grad_panel, grad_tokens
+    pieces = T // CHUNK + 1
+    return pl.pallas_call(
+        hand_over,
+        out_shape=(
+            jax.ShapeDtypeStruct((rp,), f32),
+            jax.ShapeDtypeStruct((rp, F), bf16),
+            jax.ShapeDtypeStruct((T, F), bf16),
+        ),
+        in_specs=[vmem, anywhere, anywhere],
+        out_specs=(vmem, anywhere, anywhere),
+        scratch_shapes=[V((rp, F), bf16), V((T, F), bf16), S((pieces,)), S((pieces,))],
+    )(loss, grad_panel, grad_tokens)
 
 
 def solution(mesh):

time: 76 us -> 72.2 us (0.950)
  local copies, waits for them, and re-layouts: 7.04 us -> 0 us
  Pallas kernels: 68.1 us -> 71.4 us
    unnamed x2 -> x0, local copies, waits for them, and re-layouts: 5.85 us -> none
    pallas_call x0 -> x1, Pallas kernels: none -> 4.37 us  [local(): pl.pallas_call(hand_over, out_shape=(jax.ShapeDtypeStruct((rp,), f32), ja...]
    squeeze x1 -> x0, local copies, waits for them, and re-layouts: 1.19 us -> none  [local(): return (loss[0, :rp], grad_panel, grad_tokens)]
    pallas_call x1, Pallas kernels: 68.1 us -> 67 us  [local(): pl.pallas_call(functools.partial(kernel, rows_n, cols_n), out_shape=(jax....]
where the time goes in v3:
time: 72.2 us; the launch traced here: 72 us
  Pallas kernels  71.4 us (99%)
    pallas_call x1, Pallas kernels, local(): pl.pallas_call(functools.partial(kernel, rows_n, cols_n), out_shape=(jax....  67 us
    pallas_call x1, Pallas kernels, local(): pl.pallas_call(hand_over, out_shape=(jax.ShapeDtypeStruct((rp,), f32), ja...  4.37 us

profile of v3, /device:TPU:0, one launch (start us, length us, event | category | flops | bytes accessed | tf_op | source)
XLA Modules:
  0.0 72.0 jit_solution(8072537365863271994)
XLA Ops:
  0.6 67.0 %shard_map.67 = (f32[8,128]{1,0:T(8,128)}, bf16[128,2048]{1,0:T(8,128)(2,1)}, bf16[768,2048]{1,0:T(8,128)(2,1)}) custom-call(bf16[512,2048]{1,0:T(8,128)(2,1)} %ps_h.1, bf16[512,2048]{1,0:T(8,128)(2,1)} %pt_h.1, bf16[768,2048]{1,0:T(8,128)(2,1)} %ts_h.1, bf16[768,2048]{1,0:T(8,128)(2,1)} %tt_h.1), custom_call_target="tpu_custom_call" | custom-call | tf_op jit(solution)/shard_map/pallas_call | solution.py:441
  67.7 4.4 %shard_map.68 = (f32[128]{0:T(128)}, bf16[128,2048]{1,0:T(8,128)(2,1)}, bf16[768,2048]{1,0:T(8,128)(2,1)}) custom-call(f32[8,128]{1,0:T(8,128)} %get-tuple-element.6.loss, bf16[128,2048]{1,0:T(8,128)(2,1)} %get-tuple-element.7.panel, bf16[768,2048]{1,0:T(8,128)(2,1)} %get-tuple-element.8.tokens), custom_call_target="tpu_custom_call" | custom-call | tf_op jit(solution)/shard_map/pallas_call | solution.py:456
